TPU v7x, 32 devices: a whole 2x2x4 slice. The times are simulated.
32 devices in a mesh: sec: 2 (over y), tube: 4 (over z), blk: 2 (over x), sub: 2 (over core).
Axes of the slice: x: 2, y: 2, z: 4, core: 2. Of those that a mesh axis runs over, the one named last changes fastest.
Arguments:
- latent: float32 [2048, 256], P(('sec', 'tube'), 'blk'), parts along dimension 0, may hold values from 0.2 to 5
- weight_maps: bfloat16 [8, 2048, 256], P('sub', ('sec', 'tube'), 'blk'), parts along dimension 1, may hold values from 0.039794922 to 0.19921875
- row_taps: float32 [8, 31], P('sub'), may hold values from 0.05 to 1
- col_taps: float32 [8, 31], P('sub'), may hold values from 0.05 to 1
- exposures: bfloat16 [2, 512, 128, 128], P('blk', ('sec', 'tube')), parts along dimension 1, may hold values from 0.19921875 to 5
- gains: bfloat16 [2, 512], P('blk', ('sec', 'tube')), parts along dimension 1, may hold values from 0.5 to 2
- owners: int32 [2, 512, 1], P('blk', ('sec', 'tube')), parts along dimension 1, may hold values from 0 to 3, as said below
- offsets: int32 [2, 512], P('blk', ('sec', 'tube')), parts along dimension 1, may hold values from 0 to 1, as said below
Outputs:
- updated: float32 [2048, 256], P(('sec', 'tube'), 'blk'), parts along dimension 0
There are 2 independent parts, one for each index of `sec`. A program takes and returns all parts, laid end to end along the dimension named above; an argument that names none is the same for every part. Nothing has to cross between parts.
Inputs may be any that keep to these rules, and one draw needn't show every extreme that they name: `owners`: among the 64 slots of one device no tube position is named more than 32 times; in each column of blocks some tube position is named exactly 32 times by every device of that column. `offsets`: some block places of the image receive no slot.
All inputs are finite; a program needn't handle non-finite values.
Results may differ from a plain program's by a relative error of at most 0.00035.
Values may be sent and summed in bfloat16 or wider, within the bound.
A program may use at most 64 MiB of HBM per device.

v0:
```python
import jax
import jax.numpy as jnp
from jax import lax
from jax.sharding import PartitionSpec as P


def extended(block, sides, width, periodic):
    for axis, dim in sides:
        count = lax.axis_size(axis)
        forward = [(i, i + 1) for i in range(count - 1)]
        if periodic:
            forward.append((count - 1, 0))
        backward = [(target, source) for source, target in forward]
        low = lax.ppermute(
            lax.slice_in_dim(block, block.shape[dim] - width, None, axis=dim), axis, forward
        )
        high = lax.ppermute(lax.slice_in_dim(block, 0, width, axis=dim), axis, backward)
        block = jnp.concatenate([low, block, high], axis=dim)
    return block


def sweep(source, tap_stack, length, dimension):
    running = tap_stack[0] * lax.slice_in_dim(source, 0, length, axis=dimension)
    for tap_index in range(1, tap_stack.shape[0]):
        running = running + tap_stack[tap_index] * lax.slice_in_dim(
            source, tap_index, tap_index + length, axis=dimension
        )
    return running


def separable(source, row_stack, col_stack, out_rows, out_cols):
    row_pass = sweep(source, row_stack, out_rows, source.ndim - 2)
    return sweep(row_pass, col_stack, out_cols, row_pass.ndim - 1)


def body(latent, weight_maps, row_taps, col_taps, exposures, gains, owners, offsets):
    tile_rows, block_size = latent.shape
    tap_count = row_taps.shape[1]
    margin = tap_count // 2
    row_blocks = tile_rows // block_size
    slot_count = exposures.shape[1]
    tube_count = lax.axis_size("tube")
    capacity = max(2, 2 * slot_count // tube_count)
    row_norm = row_taps / jnp.sum(row_taps, axis=1, keepdims=True)
    col_norm = col_taps / jnp.sum(col_taps, axis=1, keepdims=True)
    row_ahead = row_norm.T[:, :, None, None]
    col_ahead = col_norm.T[:, :, None, None]
    row_behind = row_norm[:, ::-1].T[:, :, None, None]
    col_behind = col_norm[:, ::-1].T[:, :, None, None]
    weight_stack = weight_maps.astype(jnp.float32)
    target = owners[0, :, 0]
    placement_plan = (offsets[0][:, None] == jnp.arange(row_blocks)[None, :]).astype(jnp.bfloat16)
    earlier = jnp.arange(slot_count)[None, :] < jnp.arange(slot_count)[:, None]
    matching = target[:, None] == target[None, :]
    order_rank = jnp.sum(matching & earlier, axis=1)
    picked_tube = (target[None, None, :] == jnp.arange(tube_count)[:, None, None]) & (
        order_rank[None, None, :] == jnp.arange(capacity)[None, :, None]
    )
    picked_tube = picked_tube.astype(jnp.bfloat16)
    send_blocks = jnp.einsum(
        "mew,wng->meng", picked_tube, exposures[0], preferred_element_type=jnp.float32
    ).astype(jnp.bfloat16)
    send_places = jnp.einsum(
        "jaf,fu->jau", picked_tube, placement_plan, preferred_element_type=jnp.float32
    ).astype(jnp.bfloat16)
    send_gains = jnp.einsum(
        "jaf,fu->jau",
        picked_tube,
        placement_plan * gains[0][:, None],
        preferred_element_type=jnp.float32,
    ).astype(jnp.bfloat16)
    got_blocks, received_positions, got_gains = (
        lax.all_to_all(send_blocks, "tube", split_axis=0, concat_axis=0, tiled=True),
        lax.all_to_all(send_places, "tube", split_axis=0, concat_axis=0, tiled=True),
        lax.all_to_all(send_gains, "tube", split_axis=0, concat_axis=0, tiled=True),
    )
    count_blocks = jnp.einsum(
        "tcr,tcxy->rxy", received_positions, got_blocks, preferred_element_type=jnp.float32
    )
    gain_blocks = jnp.sum(got_gains.astype(jnp.float32), axis=(0, 1))
    counts = count_blocks.reshape(tile_rows, block_size)
    coverage = jnp.broadcast_to(
        jnp.repeat(gain_blocks, block_size)[:, None], (tile_rows, block_size)
    )
    padded = extended(latent.astype(jnp.bfloat16), (("tube", 0),), margin, False).astype(
        latent.dtype
    )
    padded = extended(padded.astype(jnp.bfloat16), (("blk", 1),), margin, True).astype(padded.dtype)
    partial_value = jnp.sum(
        weight_stack * separable(padded[None], row_ahead, col_ahead, tile_rows, block_size), axis=0
    )
    smeared_image = lax.psum(partial_value.astype(jnp.bfloat16), "sub").astype(jnp.float32)
    quotient = counts / smeared_image
    stacked = jnp.stack([weight_stack * quotient[None], weight_stack * coverage[None]])
    weighted = extended(stacked, (("tube", 2),), margin, False)
    weighted = extended(weighted, (("blk", 3),), margin, True)
    backward = jnp.sum(separable(weighted, row_behind, col_behind, tile_rows, block_size), axis=1)
    numerator, denominator = lax.psum((backward[0], backward[1]), "sub")
    return latent * numerator / jnp.maximum(denominator, 0.25)


def solution(mesh):
    in_specs = (
        P(("sec", "tube"), "blk"),
        P("sub", ("sec", "tube"), "blk"),
        P("sub", None),
        P("sub", None),
        P("blk", ("sec", "tube"), None, None),
        P("blk", ("sec", "tube")),
        P("blk", ("sec", "tube"), None),
        P("blk", ("sec", "tube")),
    )
    out_specs = P(("sec", "tube"), "blk")
    return jax.shard_map(body, mesh=mesh, in_specs=in_specs, out_specs=out_specs, check_vma=False)
```

profile of v0, /device:TPU:0, one launch (start us, length us, event | category | flops | bytes accessed | tf_op | source)
XLA Modules:
  0.0 301.7 jit_solution(13113632499515899674)
XLA Ops:
  9.6 6.3 %all-to-all-start = ((bf16[4,32,2]{1,2,0:T(2,128)(2,1)}), bf16[4,32,2]{1,2,0:T(2,128)(2,1)S(1)}, u32[]{:S(2)}, u32[]{:S(2)}) async-start(bf16[4,32,2]{1,2,0:T(2,128)(2,1)} %convolution_convert_fusion.2), calls=%async_computation | async-start | bytes 4096 | tf_op jit(solution)/shard_map/all_to_all | solution.py:74
  17.3 4.1 %all-to-all-done = bf16[4,32,2]{1,2,0:T(2,128)(2,1)S(1)} async-done(((bf16[4,32,2]{1,2,0:T(2,128)(2,1)}), bf16[4,32,2]{1,2,0:T(2,128)(2,1)S(1)}, u32[]{:S(2)}, u32[]{:S(2)}) %all-to-all-start) | async-done | bytes 544 | tf_op jit(solution)/shard_map/all_to_all | solution.py:74
  21.4 3.2 %all-to-all-start.2 = ((bf16[4,32,2]{1,2,0:T(2,128)(2,1)}), bf16[4,32,2]{1,2,0:T(2,128)(2,1)S(1)}, u32[]{:S(2)}, u32[]{:S(2)}) async-start(bf16[4,32,2]{1,2,0:T(2,128)(2,1)} %convolution_convert_fusion.1), calls=%async_computation.2 | async-start | bytes 4096 | tf_op jit(solution)/shard_map/all_to_all | solution.py:75
  24.6 1.9 convolution_convert_fusion
  26.5 2.7 copy.88
  30.1 4.8 %all-to-all-start.1 = ((bf16[4,32,128,128]{3,1,2,0:T(8,128)(2,1)}), bf16[4,32,128,128]{3,1,2,0:T(8,128)(2,1)}, u32[]{:S(2)}, u32[]{:S(2)}) async-start(bf16[4,32,128,128]{3,1,2,0:T(8,128)(2,1)} %copy.88), calls=%async_computation.1 | async-start | bytes 8388608 | tf_op jit(solution)/shard_map/all_to_all | solution.py:73
  36.3 4.7 %collective-permute-start = (bf16[15,128]{1,0:T(8,128)(2,1)S(1)}, bf16[15,128]{1,0:T(8,128)(2,1)S(1)}, u32[]{:S(2)}, u32[]{:S(2)}) collective-permute-start(bf16[15,128]{1,0:T(8,128)(2,1)S(1)} %get-tuple-element.174), channel_id=1, source_target_pairs={{0,4},{4,8},{8,12},{1,5},{5,9},{9,13},{2,6},{6,10},{10,14},{3,7},{... | collective-permute-start | bytes 11528 | tf_op jit(solution)/shard_map/ppermute | solution.py:14
  46.6 33.9 %collective-permute-done.1 = bf16[15,128]{1,0:T(8,128)(2,1)S(1)} collective-permute-done((bf16[15,128]{1,0:T(8,128)(2,1)S(1)}, bf16[15,128]{1,0:T(8,128)(2,1)S(1)}, u32[]{:S(2)}, u32[]{:S(2)}) %collective-permute-start.1) | collective-permute-done | bytes 3872 | tf_op jit(solution)/shard_map/ppermute | solution.py:17
  80.6 20.3 %collective-permute-done = bf16[15,128]{1,0:T(8,128)(2,1)S(1)} collective-permute-done((bf16[15,128]{1,0:T(8,128)(2,1)S(1)}, bf16[15,128]{1,0:T(8,128)(2,1)S(1)}, u32[]{:S(2)}, u32[]{:S(2)}) %collective-permute-start) | collective-permute-done | bytes 3872 | tf_op jit(solution)/shard_map/ppermute | solution.py:14
  107.0 2.1 slice_bitcast_fusion.30
  145.0 1.8 copy.100
  157.4 10.0 %multiply_add_fusion = f32[4,256,158]{1,0,2:T(4,128)S(1)} fusion(f32[256,158]{0,1:T(8,128)S(1)} %copy-done.2, f32[4]{0:T(128)} %get-tuple-element.99, f32[256,158]{0,1:T(8,128)} %copy.120, f32[4]{0:T(128)} %get-tuple-element.100, f32[256,158]{0,1:T(8,128)} %copy.119, f32[4]{0:T(128)} %get-tuple-element.101, f32[256,158]{0,1:T(8,128)} %copy.118, ...), kind=kLoop, calls=%fused_computation.134 | loop fusion | flops 9869312 | bytes 5663216 | tf_op jit(solution)/shard_map/add | solution.py:25
  167.7 4.4 %fusion.62 = bf16[256,128]{0,1:T(8,128)(2,1)} fusion(bf16[4,256,128]{1,0,2:T(4,128)(2,1)S(1)} %copy.86, f32[4,256,158]{1,0,2:T(4,128)S(1)} %multiply_add_fusion, f32[4]{0:T(128)S(1)} %copy-done.15, f32[4]{0:T(128)S(1)} %copy-done.16, f32[4]{0:T(128)S(1)} %copy-done.17, f32[4]{0:T(128)S(1)} %copy-done.18, f32[4]{0:T(128)S(1)} %copy-done.19, ...), kind=kLoop, calls=%fused_computation.135 | loop fusion | flops 8355840 | bytes 16581104 | tf_op jit(solution)/shard_map/reduce_sum | solution.py:89
  172.3 2.9 convolution_bitcast_fusion
  175.3 37.7 %all-reduce.4.cloned.1.call-done = bf16[256,128]{0,1:T(8,128)(2,1)} async-done(((bf16[256,128]{0,1:T(8,128)(2,1)}), bf16[256,128]{0,1:T(8,128)(2,1)}) %all-reduce.4.cloned.1.call-update) | async-done | bytes 65552 | tf_op jit(solution)/shard_map/psum | solution.py:92
  215.8 4.8 %collective-permute-start.4 = (f32[2,4,15,128]{2,1,3,0:T(4,128)S(1)}, f32[2,4,15,128]{2,1,3,0:T(4,128)S(1)}, u32[]{:S(2)}, u32[]{:S(2)}) collective-permute-start(f32[2,4,15,128]{2,1,3,0:T(4,128)S(1)} %get-tuple-element.133), channel_id=1, source_target_pairs={{0,4},{4,8},{8,12},{1,5},{5,9},{9,13},{2,6},{6,10},{10,14},{3,7},{... | collective-permute-start | bytes 184328 | tf_op jit(solution)/shard_map/ppermute | solution.py:14
  221.0 9.6 %collective-permute-done.5 = f32[2,4,15,128]{2,1,3,0:T(4,128)S(1)} collective-permute-done((f32[2,4,15,128]{2,1,3,0:T(4,128)S(1)}, f32[2,4,15,128]{2,1,3,0:T(4,128)S(1)}, u32[]{:S(2)}, u32[]{:S(2)}) %collective-permute-start.5) | collective-permute-done | bytes 61472 | tf_op jit(solution)/shard_map/ppermute | solution.py:17
  232.0 1.8 collective-permute-start.7
  235.0 4.7 %collective-permute-done.7 = f32[2,4,286,15]{2,1,3,0:T(4,128)S(1)} collective-permute-done((f32[2,4,286,15]{2,1,3,0:T(4,128)S(1)}, f32[2,4,286,15]{2,1,3,0:T(4,128)S(1)}, u32[]{:S(2)}, u32[]{:S(2)}) %collective-permute-start.7) | collective-permute-done | bytes 137312 | tf_op jit(solution)/shard_map/ppermute | solution.py:17
  239.7 2.1 collective-permute-done.6
  241.8 2.6 pad_maximum_fusion
  244.3 20.9 %fusion.1 = f32[2,4,256,158]{2,1,3,0:T(4,128)S(1)} fusion(f32[2,4,286,158]{2,1,3,0:T(4,128)S(1)} %pad_maximum_fusion, f32[4]{0:T(128)S(1)} %get-tuple-element.37, f32[4]{0:T(128)S(1)} %get-tuple-element.38, f32[4]{0:T(128)S(1)} %get-tuple-element.39, f32[4]{0:T(128)S(1)} %get-tuple-element.40, f32[4]{0:T(128)S(1)} %get-tuple-element.41, ...), kind=kLoop, calls=%fused_computation.4 | loop fusion | flops 19738624 | bytes 41419248 | tf_op jit(solution)/shard_map/add | solution.py:25
  265.2 6.5 %fusion.32 = f32[2,256,128]{1,2,0:T(8,128)S(1)} fusion(f32[2,4,256,158]{2,1,3,0:T(4,128)S(1)} %fusion.1, f32[4]{0:T(128)S(1)} %get-tuple-element.6, f32[4]{0:T(128)S(1)} %get-tuple-element.7, f32[4]{0:T(128)S(1)} %get-tuple-element.8, f32[4]{0:T(128)S(1)} %get-tuple-element.9, f32[4]{0:T(128)S(1)} %get-tuple-element.10, f32[4]{0:T(128)S(1)} %get-tuple-element.11, ...), kind=kLoop, calls=%fused_computation.69 | loop fusion | flops 16187392 | bytes 32768496 | tf_op jit(solution)/shard_map/reduce_sum | solution.py:97
  272.6 20.5 %all-reduce.6.cloned.1.call-done = (f32[256,128]{0,1:T(8,128)}, f32[256,128]{0,1:T(8,128)}) async-done(((f32[256,128]{0,1:T(8,128)}, f32[256,128]{0,1:T(8,128)}), (f32[256,128]{0,1:T(8,128)}, f32[256,128]{0,1:T(8,128)})) %all-reduce.6.cloned.1.call-update) | async-done | bytes 262160 | tf_op jit(solution)/shard_map/psum | solution.py:98
  (152 shorter events, 73.2 us)
Async XLA Ops:
  6.5 18.1 %copy-start = (bf16[1,64,128,128]{3,2,1,0:T(8,128)(2,1)S(1)}, bf16[1,64,128,128]{3,2,1,0:T(8,128)(2,1)}, u32[]{:S(2)}) copy-start(bf16[1,64,128,128]{3,2,1,0:T(8,128)(2,1)} %param.12) | copy-start | bytes 6291460
  9.6 11.8 %all-to-all-start = ((bf16[4,32,2]{1,2,0:T(2,128)(2,1)}), bf16[4,32,2]{1,2,0:T(2,128)(2,1)S(1)}, u32[]{:S(2)}, u32[]{:S(2)}) async-start(bf16[4,32,2]{1,2,0:T(2,128)(2,1)} %convolution_convert_fusion.2), calls=%async_computation | async-start | bytes 4096 | tf_op jit(solution)/shard_map/all_to_all | solution.py:74
  21.4 8.7 %all-to-all-start.2 = ((bf16[4,32,2]{1,2,0:T(2,128)(2,1)}), bf16[4,32,2]{1,2,0:T(2,128)(2,1)S(1)}, u32[]{:S(2)}, u32[]{:S(2)}) async-start(bf16[4,32,2]{1,2,0:T(2,128)(2,1)} %convolution_convert_fusion.1), calls=%async_computation.2 | async-start | bytes 4096 | tf_op jit(solution)/shard_map/all_to_all | solution.py:75
  29.3 11.8 %copy-start.5 = (bf16[4,256,128]{2,1,0:T(8,128)(2,1)S(1)}, bf16[4,256,128]{2,1,0:T(8,128)(2,1)}, u32[]{:S(2)}) copy-start(bf16[4,256,128]{2,1,0:T(8,128)(2,1)} %param.9) | copy-start | bytes 786436
  29.3 12.0 %copy-start.6 = (f32[4,31]{1,0:T(4,128)S(1)}, f32[4,31]{1,0:T(4,128)}, u32[]{:S(2)}) copy-start(f32[4,31]{1,0:T(4,128)} %param.10) | copy-start | bytes 1492
  29.3 12.1 %copy-start.7 = (f32[4,31]{1,0:T(4,128)S(1)}, f32[4,31]{1,0:T(4,128)}, u32[]{:S(2)}) copy-start(f32[4,31]{1,0:T(4,128)} %param.11) | copy-start | bytes 1492
  30.1 142.2 %all-to-all-start.1 = ((bf16[4,32,128,128]{3,1,2,0:T(8,128)(2,1)}), bf16[4,32,128,128]{3,1,2,0:T(8,128)(2,1)}, u32[]{:S(2)}, u32[]{:S(2)}) async-start(bf16[4,32,128,128]{3,1,2,0:T(8,128)(2,1)} %copy.88), calls=%async_computation.1 | async-start | bytes 8388608 | tf_op jit(solution)/shard_map/all_to_all | solution.py:73
  34.9 178.1 %all-reduce.4.cloned.1.call-start = ((), (), s32[]{:S(2)}) async-start(), calls=%async_computation.3 | async-start | bytes 131072 | tf_op jit(solution)/shard_map/psum | solution.py:92
  35.0 45.5 %collective-permute-start.1 = (bf16[15,128]{1,0:T(8,128)(2,1)S(1)}, bf16[15,128]{1,0:T(8,128)(2,1)S(1)}, u32[]{:S(2)}, u32[]{:S(2)}) collective-permute-start(bf16[15,128]{1,0:T(8,128)(2,1)S(1)} %get-tuple-element.175), channel_id=1, source_target_pairs={{4,0},{8,4},{12,8},{5,1},{9,5},{13,9},{6,2},{10,6},{14,10},{7,3},{... | collective-permute-start | bytes 11528 | tf_op jit(solution)/shard_map/ppermute | solution.py:17
  36.3 64.5 %collective-permute-start = (bf16[15,128]{1,0:T(8,128)(2,1)S(1)}, bf16[15,128]{1,0:T(8,128)(2,1)S(1)}, u32[]{:S(2)}, u32[]{:S(2)}) collective-permute-start(bf16[15,128]{1,0:T(8,128)(2,1)S(1)} %get-tuple-element.174), channel_id=1, source_target_pairs={{0,4},{4,8},{8,12},{1,5},{5,9},{9,13},{2,6},{6,10},{10,14},{3,7},{... | collective-permute-start | bytes 11528 | tf_op jit(solution)/shard_map/ppermute | solution.py:14
  101.0 4.4 %collective-permute-start.3 = (bf16[286,15]{1,0:T(8,128)(2,1)S(1)}, bf16[286,15]{1,0:T(8,128)(2,1)S(1)}, u32[]{:S(2)}, u32[]{:S(2)}) collective-permute-start(bf16[286,15]{1,0:T(8,128)(2,1)S(1)} %get-tuple-element.171), channel_id=1, source_target_pairs={{2,0},{0,2},{3,1},{1,3},{6,4},{4,6},{7,5},{5,7},{10,8},{8,10},{11,... | collective-permute-start | bytes 25748 | tf_op jit(solution)/shard_map/ppermute | solution.py:17
  102.6 4.4 %collective-permute-start.2 = (bf16[286,15]{1,0:T(8,128)(2,1)S(1)}, bf16[286,15]{1,0:T(8,128)(2,1)S(1)}, u32[]{:S(2)}, u32[]{:S(2)}) collective-permute-start(bf16[286,15]{1,0:T(8,128)(2,1)S(1)} %get-tuple-element.170), channel_id=1, source_target_pairs={{0,2},{2,0},{1,3},{3,1},{4,6},{6,4},{5,7},{7,5},{8,10},{10,8},{9,1... | collective-permute-start | bytes 25748 | tf_op jit(solution)/shard_map/ppermute | solution.py:14
  145.0 10.4 %copy-start.1 = (f32[256,158]{1,0:T(8,128)S(1)}, f32[256,158]{1,0:T(8,128)}, u32[]{:S(2)}) copy-start(f32[256,158]{1,0:T(8,128)} %get-tuple-element.164) | copy-start | bytes 485380
  157.2 10.3 %copy-start.8 = (f32[4]{0:T(128)S(1)}, f32[4]{0:T(128)}, u32[]{:S(2)}) copy-start(f32[4]{0:T(128)} %get-tuple-element.92) | copy-start | bytes 52
  157.2 10.3 %copy-start.9 = (f32[4]{0:T(128)S(1)}, f32[4]{0:T(128)}, u32[]{:S(2)}) copy-start(f32[4]{0:T(128)} %get-tuple-element.93) | copy-start | bytes 52
  157.2 10.3 %copy-start.10 = (f32[4]{0:T(128)S(1)}, f32[4]{0:T(128)}, u32[]{:S(2)}) copy-start(f32[4]{0:T(128)} %get-tuple-element.94) | copy-start | bytes 52
  157.2 10.3 %copy-start.11 = (f32[4]{0:T(128)S(1)}, f32[4]{0:T(128)}, u32[]{:S(2)}) copy-start(f32[4]{0:T(128)} %get-tuple-element.95) | copy-start | bytes 52
  157.2 10.3 %copy-start.12 = (f32[4]{0:T(128)S(1)}, f32[4]{0:T(128)}, u32[]{:S(2)}) copy-start(f32[4]{0:T(128)} %get-tuple-element.96) | copy-start | bytes 52
  172.2 41.7 %copy-start.33 = (f32[256]{0:T(256)S(1)}, f32[256]{0:T(256)}, u32[]{:S(2)}) copy-start(f32[256]{0:T(256)} %broadcast_bitcast_fusion) | copy-start | bytes 3076
  172.2 120.9 %all-reduce.6.cloned.1.call-start = ((), (), s32[]{:S(2)}) async-start(), calls=%async_computation.4 | async-start | bytes 524288 | tf_op jit(solution)/shard_map/psum | solution.py:98
  214.5 16.0 %collective-permute-start.5 = (f32[2,4,15,128]{2,1,3,0:T(4,128)S(1)}, f32[2,4,15,128]{2,1,3,0:T(4,128)S(1)}, u32[]{:S(2)}, u32[]{:S(2)}) collective-permute-start(f32[2,4,15,128]{2,1,3,0:T(4,128)S(1)} %get-tuple-element.134), channel_id=1, source_target_pairs={{4,0},{8,4},{12,8},{5,1},{9,5},{13,9},{6,2},{10,6},{14,10},{7,3},{... | collective-permute-start | bytes 184328 | tf_op jit(solution)/shard_map/ppermute | solution.py:17
  215.8 15.9 %collective-permute-start.4 = (f32[2,4,15,128]{2,1,3,0:T(4,128)S(1)}, f32[2,4,15,128]{2,1,3,0:T(4,128)S(1)}, u32[]{:S(2)}, u32[]{:S(2)}) collective-permute-start(f32[2,4,15,128]{2,1,3,0:T(4,128)S(1)} %get-tuple-element.133), channel_id=1, source_target_pairs={{0,4},{4,8},{8,12},{1,5},{5,9},{9,13},{2,6},{6,10},{10,14},{3,7},{... | collective-permute-start | bytes 184328 | tf_op jit(solution)/shard_map/ppermute | solution.py:14
  232.0 7.6 %collective-permute-start.7 = (f32[2,4,286,15]{2,1,3,0:T(4,128)S(1)}, f32[2,4,286,15]{2,1,3,0:T(4,128)S(1)}, u32[]{:S(2)}, u32[]{:S(2)}) collective-permute-start(f32[2,4,286,15]{2,1,3,0:T(4,128)S(1)} %get-tuple-element.132), channel_id=1, source_target_pairs={{2,0},{0,2},{3,1},{1,3},{6,4},{4,6},{7,5},{5,7},{10,8},{8,10},{11,... | collective-permute-start | bytes 411848 | tf_op jit(solution)/shard_map/ppermute | solution.py:17
  233.8 8.0 %collective-permute-start.6 = (f32[2,4,286,15]{2,1,3,0:T(4,128)S(1)}, f32[2,4,286,15]{2,1,3,0:T(4,128)S(1)}, u32[]{:S(2)}, u32[]{:S(2)}) collective-permute-start(f32[2,4,286,15]{2,1,3,0:T(4,128)S(1)} %get-tuple-element.131), channel_id=1, source_target_pairs={{0,2},{2,0},{1,3},{3,1},{4,6},{6,4},{5,7},{7,5},{8,10},{10,8},{9,1... | collective-permute-start | bytes 411848 | tf_op jit(solution)/shard_map/ppermute | solution.py:14
  (23 other events, 220.1 us)
Sparse Core Ops, SparseCore 0:
  172.3 40.6 all-reduce.3
  272.6 20.4 all-reduce.5
where the time goes:
time: 303 us; the launch traced here: 302 us
  waiting for transfers between devices  138 us (46%)
  local copies, waits for them, and re-layouts  61.5 us (20%)
  other arithmetic  49.7 us (16%)
  starting transfers between devices  30.7 us (10%)
  between operations  14.1 us (5%)
  matrix products  7.66 us (3%)
    ppermute x4, waiting for transfers between devices, extended(): lax.ppermute(lax.slice_in_dim(block, 0, width, axis=dim), axis, backward)  49.9 us
    mul x31, local copies, waits for them, and re-layouts, sweep(): tap_stack[tap_index]  47.9 us
    psum x1, waiting for transfers between devices, body(): lax.psum(partial_value.astype(jnp.bfloat16), 'sub').astype(jnp.float32)  37.7 us
    add x2, other arithmetic, sweep(): running + tap_stack[tap_index] * lax.slice_in_dim(source, tap_index, tap_...  30.9 us
    ppermute x4, waiting for transfers between devices, extended(): lax.ppermute(lax.slice_in_dim(block, block.shape[dim] - width, None, axis...  25.1 us
    psum x1, waiting for transfers between devices, body(): numerator, denominator = lax.psum((backward[0], backward[1]), 'sub')  20.5 us
    ppermute x4, starting transfers between devices, extended(): lax.ppermute(lax.slice_in_dim(block, block.shape[dim] - width, None, axis...  10.4 us
    reduce_sum x1, other arithmetic, body(): jnp.sum(separable(weighted, row_behind, col_behind, tile_rows, block_size...  6.54 us
  transfers between devices with their start and end apart: 13, of which 12 were waited for; matrix products, arithmetic and copies ran while one was open for 27% of the time, Pallas kernels for 0%

commit v1 on v0

v1 whole, which is shorter than its diff:
```python
import functools

import jax
import jax.numpy as jnp
from jax import lax
from jax.experimental import pallas as pl
from jax.experimental.pallas import tpu as pltpu
from jax.sharding import PartitionSpec as P

MESH = pl.DeviceIdType.MESH
F32 = jnp.float32
BF16 = jnp.bfloat16
HALO = 16
PACK = 3
CHUNK = 8


def dot(a, b):
    return jnp.dot(a, b, preferred_element_type=F32)


def band(base, shift, rows):
    wide = jnp.broadcast_to(base, (rows, base.shape[1]))
    return pltpu.roll(wide, shift, 1, stride=1, stride_axis=0)


def kernel(
    tubes,
    blks,
    latent_ref,
    weight_ref,
    row_ref,
    col_ref,
    exposure_ref,
    gain_ref,
    owner_ref,
    offset_ref,
    out_ref,
    exposure_buf,
    latent_half,
    view,
    side_view,
    weight_other,
    tap_own,
    tap_other,
    gain_send,
    gain_recv,
    mask,
    count_send,
    count_recv,
    row_band,
    row_band_t,
    col_band,
    scaled,
    spread,
    main_send,
    strip_send,
    packed_send,
    main_recv,
    edge_recv,
    packed_recv,
    corner_recv,
    total,
    load_sem,
    view_send,
    view_recv,
    weight_sem,
    tap_sem,
    gain_ssem,
    gain_rsem,
    count_ssem,
    count_rsem,
    field_ssem,
    main_rsem,
    edge_rsem,
    packed_rsem,
    corner_rsem,
):
    rows, block = latent_ref.shape
    half = rows // 2
    ext = half + 2 * HALO
    inner = half + HALO
    group = inner // PACK
    kernels = weight_ref.shape[0]
    taps = row_ref.shape[1]
    margin = taps // 2
    slots = exposure_ref.shape[0]
    t = lax.axis_index("tube")
    b = lax.axis_index("blk")
    s = lax.axis_index("sub")
    o = 1 - s
    sides = (1,) if blks == 2 else (1, -1)
    ahead = t + 1 - 2 * s
    behind = t - 1 + 2 * s
    has_ahead = (ahead >= 0) & (ahead < tubes)
    has_behind = (behind >= 0) & (behind < tubes)

    def blk_at(step):
        return lax.rem(b + step + blks, blks)

    def at(tube=None, blk=None, sub=None):
        return {
            "tube": t if tube is None else tube,
            "blk": b if blk is None else blk,
            "sub": s if sub is None else sub,
        }

    def remote(src, dst, ssem, rsem, device):
        return pltpu.make_async_remote_copy(
            src_ref=src,
            dst_ref=dst,
            send_sem=ssem,
            recv_sem=rsem,
            device_id=device,
            device_id_type=MESH,
        )

    loads = [
        pltpu.make_async_copy(
            exposure_ref.at[pl.ds(c * CHUNK, CHUNK)],
            exposure_buf.at[pl.ds(c * CHUNK, CHUNK)],
            load_sem.at[c],
        )
        for c in range(slots // CHUNK)
    ]
    for load in loads:
        load.start()

    barrier = pltpu.get_barrier_semaphore()
    near = [0] + list(sides)
    fixed = 0
    for step in near:
        for sub in (s, o):
            if step == 0 and sub is s:
                continue
            pl.semaphore_signal(barrier, inc=1, device_id=at(blk=blk_at(step), sub=sub), device_id_type=MESH)
            fixed += 1
    for j in range(1, tubes):
        pl.semaphore_signal(
            barrier, inc=1, device_id=at(tube=lax.rem(t + j, tubes)), device_id_type=MESH
        )
        fixed += 1
    extra = 2 * len(near) - 1
    for beside in (t - 1, t + 1):

        @pl.when((beside >= 0) & (beside < tubes))
        def _():
            for step in near:
                for sub in (s, o):
                    if step == 0 and sub is s:
                        continue
                    pl.semaphore_signal(
                        barrier,
                        inc=1,
                        device_id=at(tube=beside, blk=blk_at(step), sub=sub),
                        device_id_type=MESH,
                    )

    latent_half[...] = latent_ref[...].astype(BF16)
    tap_own[...] = jnp.zeros_like(tap_own)
    tap_own[0:kernels, 0:taps] = row_ref[...]
    tap_own[kernels : 2 * kernels, 0:taps] = col_ref[...]
    eye = lax.broadcasted_iota(jnp.int32, (slots, slots), 0) == lax.broadcasted_iota(
        jnp.int32, (slots, slots), 1
    )
    offset = jnp.sum(
        jnp.where(eye, jnp.broadcast_to(offset_ref[...].astype(F32), (slots, slots)), 0.0),
        axis=1,
        keepdims=True,
    )
    gain = jnp.sum(
        jnp.where(eye, jnp.broadcast_to(gain_ref[...].astype(F32), (slots, slots)), 0.0),
        axis=1,
        keepdims=True,
    )
    owner = owner_ref[...].astype(F32)
    here = s.astype(F32)
    for p in range(tubes):
        hit = jnp.where((owner == float(p)) & (offset == here), 1.0, 0.0)
        mask[p] = jnp.broadcast_to(hit, (slots, block))
        gain_send[p] = jnp.broadcast_to(jnp.sum(hit * gain, axis=0, keepdims=True), (8, block))

    pl.semaphore_wait(
        barrier,
        fixed + extra * ((t > 0).astype(jnp.int32) + (t < tubes - 1).astype(jnp.int32)),
    )

    tap_copy = remote(tap_own, tap_other, tap_sem.at[0], tap_sem.at[1], at(sub=o))
    tap_copy.start()
    weight_copy = remote(
        weight_ref.at[:, pl.ds(o * half, half)],
        weight_other,
        weight_sem.at[0],
        weight_sem.at[1],
        at(sub=o),
    )
    weight_copy.start()
    gain_copies = []
    for j in range(1, tubes):
        p = lax.rem(t + j, tubes)
        gain_copies.append(
            remote(gain_send.at[p], gain_recv.at[j - 1], gain_ssem.at[j - 1], gain_rsem.at[j - 1], at(tube=p))
        )
        gain_copies[-1].start()
    own_rows = pl.ds(pl.multiple_of(s * (rows - inner), HALO), inner)
    own_place = pl.ds(pl.multiple_of(o * HALO, HALO), inner)
    edge_rows = pl.ds(pl.multiple_of(o * (rows - HALO), HALO), HALO)
    edge_place = pl.ds(pl.multiple_of(s * inner, HALO), HALO)
    edge_copies = [
        remote(
            latent_half.at[edge_rows],
            view.at[edge_place],
            view_send.at[0],
            view_recv.at[0],
            at(tube=ahead),
        )
    ]
    side_copies = []
    for i, step in enumerate(sides):
        side_copies.append(
            remote(
                latent_half.at[own_rows],
                side_view.at[i, own_place],
                view_send.at[1 + 2 * i],
                view_recv.at[1 + 2 * i],
                at(blk=blk_at(step)),
            )
        )
        edge_copies.append(
            remote(
                latent_half.at[edge_rows],
                side_view.at[i, edge_place],
                view_send.at[2 + 2 * i],
                view_recv.at[2 + 2 * i],
                at(tube=ahead, blk=blk_at(step)),
            )
        )
    for copy in side_copies:
        copy.start()

    @pl.when(has_ahead)
    def _():
        for copy in edge_copies:
            copy.start()

    view[own_place, :] = latent_half[own_rows, :]
    piece = half // 2
    count_copies = []
    for h in range(2):
        for low in range(0, tubes, 4):
            places = range(low, min(low + 4, tubes))

            def add(c, accs, h=h, places=places, wait=(h == 0 and low == 0)):
                base = pl.multiple_of(c * CHUNK, CHUNK)
                if wait:
                    pltpu.make_async_copy(
                        exposure_ref.at[pl.ds(base, CHUNK)],
                        exposure_buf.at[pl.ds(base, CHUNK)],
                        load_sem.at[c],
                    ).wait()
                picks = [mask[p, pl.ds(base, CHUNK), :] for p in places]
                for q in range(CHUNK):
                    value = exposure_buf[base + q, h * piece : (h + 1) * piece, :].astype(F32)
                    accs = tuple(a + m[q : q + 1, :] * value for a, m in zip(accs, picks))
                return accs

            sums = lax.fori_loop(
                0, slots // CHUNK, add, tuple(jnp.zeros((piece, block), F32) for _ in places)
            )
            for p, value in zip(places, sums):
                count_send[p, h * piece : (h + 1) * piece, :] = value.astype(BF16)
        for j in range(1, tubes):
            p = lax.rem(t + j, tubes)
            part = pl.ds(h * piece, piece)
            count_copies.append(
                remote(
                    count_send.at[p, part],
                    count_recv.at[j - 1, part],
                    count_ssem.at[h, j - 1],
                    count_rsem.at[h, j - 1],
                    at(tube=p),
                )
            )
            count_copies[-1].start()

    tap_copy.wait()
    for i, ref in enumerate((tap_own, tap_other)):
        rounded = ref[...].astype(BF16).astype(F32)
        sums = jnp.sum(rounded, axis=1, keepdims=True)
        scale = 1.0 / (sums[0:kernels] * sums[kernels : 2 * kernels])
        if i == 1:
            weight_copy.wait()
        for k in range(kernels):
            n = i * kernels + k
            along = band(rounded[k : k + 1], HALO - margin, half)
            around = band(rounded[kernels + k : kernels + k + 1], 2 * block - margin, block)
            row_band[n] = along.astype(BF16)
            row_band_t[:, n * half : (n + 1) * half] = along.T[0:ext].astype(BF16)
            col_band[n] = around.astype(BF16)
            if i == 0:
                own = weight_ref[k, pl.ds(pl.multiple_of(s * half, half), half), :]
            else:
                own = weight_other[k]
            scaled[n] = own.astype(F32) * scale[k : k + 1]

    def adjoint(factor):
        for n in range(2 * kernels):
            term = scaled[n] if factor is None else scaled[n] * factor
            spread[n * half : (n + 1) * half, :] = dot(term.astype(BF16), col_band[n]).astype(BF16)
        return dot(row_band_t[...], spread[...])

    lane = lax.broadcasted_iota(jnp.int32, (1, block), 1)
    if blks == 2:
        lanes_of = [(lane < HALO) | (lane >= block - HALO)]
    else:
        lanes_of = [lane < HALO, lane >= block - HALO]

    def exchange(f, value):
        main_send[f] = value[:, 0:block]
        strip_send[f] = value[:, block : 2 * block]
        packed = jnp.zeros((group, block), F32)
        start = pl.multiple_of(o * HALO, HALO)
        for g in range(PACK):
            packed = packed + pltpu.roll(
                strip_send[f, pl.ds(start + g * group, group), :], HALO + 2 * HALO * g, 1
            )
        packed_send[f] = packed
        copies, edges = [], []
        count = 0

        def add(to, src, dst, rsem, device):
            nonlocal count
            to.append(remote(src, dst, field_ssem.at[f, count], rsem, device))
            count += 1

        for i, step in enumerate(sides):
            for sub in (s, o):
                add(
                    copies,
                    packed_send.at[f],
                    packed_recv.at[f, i, s],
                    packed_rsem.at[f, i, s],
                    at(blk=blk_at(step), sub=sub),
                )
                add(
                    edges,
                    strip_send.at[f, edge_place],
                    corner_recv.at[f, i, o],
                    corner_rsem.at[f, i, o],
                    at(tube=behind, blk=blk_at(step), sub=sub),
                )
        for sub in (s, o):
            add(
                edges,
                main_send.at[f, edge_place],
                edge_recv.at[f, o],
                edge_rsem.at[f, o],
                at(tube=behind, sub=sub),
            )
        add(copies, main_send.at[f, own_place], main_recv.at[f], main_rsem.at[f], at(sub=o))
        for copy in copies:
            copy.start()

        @pl.when(has_behind)
        def _():
            for copy in edges:
                copy.start()

        return copies, edges

    def landed(buf, rsem):
        remote(buf, buf, rsem, rsem, at(sub=o)).wait_recv()

    def collect(f):
        other_rows = pl.ds(pl.multiple_of(o * (rows - inner), HALO), inner)
        total[f, edge_rows, :] = jnp.zeros((HALO, block), F32)
        total[f, pl.ds(pl.multiple_of(o * inner, HALO), rows - inner), :] = jnp.zeros(
            (rows - inner, block), F32
        )
        total[f, own_rows, :] = main_send[f, own_place, :]
        landed(main_recv.at[f], main_rsem.at[f])
        total[f, other_rows, :] += main_recv[f]
        for i in range(len(sides)):
            for sub in range(2):
                landed(packed_recv.at[f, i, sub], packed_rsem.at[f, i, sub])
                for g in range(PACK):
                    value = pltpu.roll(
                        packed_recv[f, i, sub], block - (HALO + 2 * HALO * g) % block, 1
                    )
                    start = sub * (rows - inner) + g * group
                    total[f, start : start + group, :] += jnp.where(lanes_of[i], value, 0.0)
        for n, (cond, start) in enumerate(((t > 0, 0), (t < tubes - 1, rows - HALO))):

            @pl.when(cond)
            def _():
                landed(edge_recv.at[f, n], edge_rsem.at[f, n])
                value = edge_recv[f, n]
                for i in range(len(sides)):
                    landed(corner_recv.at[f, i, n], corner_rsem.at[f, i, n])
                    value = value + jnp.where(lanes_of[i], corner_recv[f, i, n], 0.0)
                total[f, start : start + HALO, :] += value

    for copy in side_copies:
        copy.wait_recv()

    @pl.when(has_behind)
    def _():
        for copy in edge_copies:
            copy.wait_recv()

    @pl.when(jnp.logical_not(has_behind))
    def _():
        view[edge_place, :] = jnp.zeros((HALO, block), BF16)
        for i in range(len(sides)):
            side_view[i, edge_place, :] = jnp.zeros((HALO, block), BF16)

    if blks == 2:
        beside = side_view[0]
    else:
        beside = jnp.where(lane < block // 2, side_view[1], side_view[0])
    seen = jnp.concatenate([view[...], beside], axis=1)
    seen = jnp.concatenate([seen, jnp.zeros((2 * block - ext, 2 * block), BF16)], axis=0)
    blurred = jnp.zeros((half, block), F32)
    for n in range(2 * kernels):
        along = dot(row_band[n], seen).astype(BF16)
        both = lax.dot_general(
            along, col_band[n], (((1,), (1,)), ((), ())), preferred_element_type=F32
        )
        blurred = blurred + scaled[n] * both
    inverse = 1.0 / blurred

    coverage = gain_send[t]
    for j, copy in enumerate(gain_copies):
        copy.wait()
        coverage = coverage + gain_recv[j]
    sent_d = exchange(0, adjoint(None) * coverage[0:1, 0:1])
    counts_own = count_send[t].astype(F32)
    collect(0)

    for copy in count_copies:
        copy.wait()
    counts = counts_own
    for j in range(tubes - 1):
        counts = counts + count_recv[j].astype(F32)
    sent_n = exchange(1, adjoint(counts * inverse))
    collect(1)
    out_ref[...] = latent_ref[...] * total[1] / jnp.maximum(total[0], 0.25)

    for copy in side_copies:
        copy.wait_send()

    @pl.when(has_ahead)
    def _():
        for copy in edge_copies:
            copy.wait_send()

    for copies, edges in (sent_d, sent_n):
        for copy in copies:
            copy.wait_send()

        @pl.when(has_behind)
        def _():
            for copy in edges:
                copy.wait_send()


def body(tubes, blks, latent, weight_maps, row_taps, col_taps, exposures, gains, owners, offsets):
    rows, block = latent.shape
    half = rows // 2
    ext = half + 2 * HALO
    inner = half + HALO
    kernels = weight_maps.shape[0]
    slots = exposures.shape[1]
    nside = 1 if blks == 2 else 2
    peers = tubes - 1
    vmem = pl.BlockSpec(memory_space=pltpu.VMEM)
    dma = pltpu.SemaphoreType.DMA
    return pl.pallas_call(
        functools.partial(kernel, tubes, blks),
        out_shape=jax.ShapeDtypeStruct((rows, block), F32),
        in_specs=[vmem] * 4 + [pl.BlockSpec(memory_space=pl.ANY)] + [vmem] * 3,
        out_specs=vmem,
        scratch_shapes=[
            pltpu.VMEM((slots, block, block), BF16),
            pltpu.VMEM((rows, block), BF16),
            pltpu.VMEM((ext, block), BF16),
            pltpu.VMEM((nside, ext, block), BF16),
            pltpu.VMEM((kernels, half, block), BF16),
            pltpu.VMEM((2 * kernels, 2 * block), F32),
            pltpu.VMEM((2 * kernels, 2 * block), F32),
            pltpu.VMEM((tubes, 8, block), F32),
            pltpu.VMEM((peers, 8, block), F32),
            pltpu.VMEM((tubes, slots, block), F32),
            pltpu.VMEM((tubes, half, block), BF16),
            pltpu.VMEM((peers, half, block), BF16),
            pltpu.VMEM((2 * kernels, half, 2 * block), BF16),
            pltpu.VMEM((ext, 2 * kernels * half), BF16),
            pltpu.VMEM((2 * kernels, block, 2 * block), BF16),
            pltpu.VMEM((2 * kernels, half, block), F32),
            pltpu.VMEM((2 * kernels * half, 2 * block), BF16),
            pltpu.VMEM((2, ext, block), F32),
            pltpu.VMEM((2, ext, block), F32),
            pltpu.VMEM((2, inner // PACK, block), F32),
            pltpu.VMEM((2, inner, block), F32),
            pltpu.VMEM((2, 2, HALO, block), F32),
            pltpu.VMEM((2, nside, 2, inner // PACK, block), F32),
            pltpu.VMEM((2, nside, 2, HALO, block), F32),
            pltpu.VMEM((2, rows, block), F32),
            dma((slots // CHUNK,)),
            dma((1 + 2 * nside,)),
            dma((1 + 2 * nside,)),
            dma((2,)),
            dma((2,)),
            dma((peers,)),
            dma((peers,)),
            dma((2, peers)),
            dma((2, peers)),
            dma((2, 4 * nside + 3)),
            dma((2,)),
            dma((2, 2)),
            dma((2, nside, 2)),
            dma((2, nside, 2)),
        ],
        compiler_params=pltpu.CompilerParams(
            collective_id=0, has_side_effects=True, vmem_limit_bytes=40 * 1024 * 1024
        ),
    )(latent, weight_maps, row_taps, col_taps, exposures[0], gains, owners[0], offsets)


def solution(mesh):
    in_specs = (
        P(("sec", "tube"), "blk"),
        P("sub", ("sec", "tube"), "blk"),
        P("sub", None),
        P("sub", None),
        P("blk", ("sec", "tube"), None, None),
        P("blk", ("sec", "tube")),
        P("blk", ("sec", "tube"), None),
        P("blk", ("sec", "tube")),
    )
    out_specs = P(("sec", "tube"), "blk")
    run = functools.partial(body, mesh.shape["tube"], mesh.shape["blk"])
    return jax.shard_map(run, mesh=mesh, in_specs=in_specs, out_specs=out_specs, check_vma=False)
```

time: 303 us -> 25.6 us (0.08)
  waiting for transfers between devices: 138 us -> 0 us
  local copies, waits for them, and re-layouts: 61.5 us -> 7.52 us
  other arithmetic: 49.7 us -> 0 us
  starting transfers between devices: 30.7 us -> 0 us
  Pallas kernels: 0 us -> 17.8 us
  between operations: 14.1 us -> 0.02 us
  matrix products: 7.66 us -> 0 us
    ppermute x8 -> x0, waiting for transfers between devices: 75 us -> none  [the longest x4 49.9 us: extended(): lax.ppermute(lax.slice_in_dim(block, 0, width, axis=dim), axis, backward)]
    psum x2 -> x0, waiting for transfers between devices: 58.3 us -> none  [the longest x1 37.7 us: body(): lax.psum(partial_value.astype(jnp.bfloat16), 'sub').astype(jnp.float32)]
    mul x33 -> x0, local copies, waits for them, and re-layouts: 50.1 us -> none  [the longest x31 47.9 us: sweep(): tap_stack[tap_index]]
    add x2 -> x0, other arithmetic: 30.9 us -> none  [sweep(): running + tap_stack[tap_index] * lax.slice_in_dim(source, tap_index, tap_...]
    pallas_call x0 -> x1, Pallas kernels: none -> 17.8 us  [body(): pl.pallas_call(functools.partial(kernel, tubes, blks), out_shape=jax.Shap...]
    ppermute x8 -> x0, starting transfers between devices: 16.3 us -> none  [the longest x4 10.4 us: extended(): lax.ppermute(lax.slice_in_dim(block, block.shape[dim] - width, None, axis...]
    all_to_all x3 -> x0, starting transfers between devices: 14.3 us -> none  [the longest x1 6.32 us: body(): lax.all_to_all(send_places, 'tube', split_axis=0, concat_axis=0, tiled=True)]
    reduce_sum x6 -> x0, other arithmetic: 12.3 us -> none  [the longest x1 6.54 us: body(): jnp.sum(separable(weighted, row_behind, col_behind, tile_rows, block_size...]
  transfers between devices with their start and end apart: 13 -> 0, of which waited for: 12 -> 0; matrix products, arithmetic and copies ran while one was open for 27% -> 0% of each run, Pallas kernels for 0% -> 0%
where the time goes in v1:
time: 25.6 us; the launch traced here: 25.3 us
  Pallas kernels  17.8 us (70%)
  local copies, waits for them, and re-layouts  7.52 us (29%)
    pallas_call x1, Pallas kernels, body(): pl.pallas_call(functools.partial(kernel, tubes, blks), out_shape=jax.Shap...  17.8 us
    unnamed x15, local copies, waits for them, and re-layouts  6.77 us
    squeeze x1, local copies, waits for them, and re-layouts, body(): owners[0]  0.74 us

profile of v1, /device:TPU:0, one launch (start us, length us, event | category | flops | bytes accessed | tf_op | source)
XLA Modules:
  0.0 25.3 jit_solution(2718333591800787995)
XLA Ops:
  0.0 0.7 %copy.9.owner_ref = s32[64,1]{1,0:T(8,128)S(1)} copy(s32[64,1]{0,1:T(1,128)} %bitcast.3) | data formatting | bytes 512 | tf_op jit(solution)/shard_map/squeeze | solution.py:527
  0.7 0.0 copy-start
  0.7 1.6 %copy-done = bf16[1,64,128,128]{3,2,1,0:T(8,128)(2,1)S(1)} copy-done((bf16[1,64,128,128]{3,2,1,0:T(8,128)(2,1)S(1)}, bf16[1,64,128,128]{3,2,1,0:T(8,128)(2,1)}, u32[]{:S(2)}) %copy-start) | copy-done | bytes 2097176
  2.3 0.0 copy-start.1
  2.3 0.9 %copy-done.1 = bf16[4,256,128]{2,1,0:T(8,128)(2,1)S(1)} copy-done((bf16[4,256,128]{2,1,0:T(8,128)(2,1)S(1)}, bf16[4,256,128]{2,1,0:T(8,128)(2,1)}, u32[]{:S(2)}) %copy-start.1) | copy-done | bytes 262168
  3.3 0.0 copy-start.2
  3.3 0.9 %copy-done.2 = f32[256,128]{1,0:T(8,128)S(1)} copy-done((f32[256,128]{1,0:T(8,128)S(1)}, f32[256,128]{1,0:T(8,128)}, u32[]{:S(2)}) %copy-start.2) | copy-done | bytes 131096
  4.2 0.0 copy-start.3
  4.2 0.7 %copy-done.3 = f32[4,31]{1,0:T(4,128)S(1)} copy-done((f32[4,31]{1,0:T(4,128)S(1)}, f32[4,31]{1,0:T(4,128)}, u32[]{:S(2)}) %copy-start.3) | copy-done | bytes 520
  4.9 0.0 copy-start.4
  4.9 0.7 %copy-done.4 = f32[4,31]{1,0:T(4,128)S(1)} copy-done((f32[4,31]{1,0:T(4,128)S(1)}, f32[4,31]{1,0:T(4,128)}, u32[]{:S(2)}) %copy-start.4) | copy-done | bytes 520
  5.6 0.0 copy-start.5
  5.6 0.7 %copy-done.5 = bf16[1,64]{1,0:T(2,128)(2,1)S(1)} copy-done((bf16[1,64]{1,0:T(2,128)(2,1)S(1)}, bf16[1,64]{1,0:T(2,128)(2,1)}, u32[]{:S(2)}) %copy-start.5) | copy-done | bytes 152
  6.2 0.0 copy-start.6
  6.2 0.7 %copy-done.6 = s32[1,64]{1,0:T(1,128)S(1)} copy-done((s32[1,64]{1,0:T(1,128)S(1)}, s32[1,64]{1,0:T(1,128)}, u32[]{:S(2)}) %copy-start.6) | copy-done | bytes 280
  6.9 17.8 %shard_map.82 = f32[256,128]{1,0:T(8,128)S(1)} custom-call(f32[256,128]{1,0:T(8,128)S(1)} %copy-done.2, bf16[4,256,128]{2,1,0:T(8,128)(2,1)S(1)} %copy-done.1, f32[4,31]{1,0:T(4,128)S(1)} %copy-done.3, f32[4,31]{1,0:T(4,128)S(1)} %copy-done.4, bf16[64,128,128]{2,1,0:T(8,128)(2,1)S(1)} %bitcast.2, bf16[1,64]{1,0:T(2,128)(2,1)S(1)} %copy-done.5, ...), custom_call_target="tpu_custom_call" | custom-call | tf_op jit(solution)/shard_map/pallas_call | solution.py:478
  24.7 0.7 %copy.11 = f32[256,128]{1,0:T(8,128)} copy(f32[256,128]{1,0:T(8,128)S(1)} %shard_map.82) | data formatting | bytes 262144
Async XLA Ops:
  0.7 1.6 %copy-start = (bf16[1,64,128,128]{3,2,1,0:T(8,128)(2,1)S(1)}, bf16[1,64,128,128]{3,2,1,0:T(8,128)(2,1)}, u32[]{:S(2)}) copy-start(bf16[1,64,128,128]{3,2,1,0:T(8,128)(2,1)} %param.12) | copy-start | bytes 6291460
  2.3 0.9 %copy-start.1 = (bf16[4,256,128]{2,1,0:T(8,128)(2,1)S(1)}, bf16[4,256,128]{2,1,0:T(8,128)(2,1)}, u32[]{:S(2)}) copy-start(bf16[4,256,128]{2,1,0:T(8,128)(2,1)} %weight_ref.1) | copy-start | bytes 786436
  3.3 0.9 %copy-start.2 = (f32[256,128]{1,0:T(8,128)S(1)}, f32[256,128]{1,0:T(8,128)}, u32[]{:S(2)}) copy-start(f32[256,128]{1,0:T(8,128)} %latent_ref.1) | copy-start | bytes 393220
  4.2 0.7 %copy-start.3 = (f32[4,31]{1,0:T(4,128)S(1)}, f32[4,31]{1,0:T(4,128)}, u32[]{:S(2)}) copy-start(f32[4,31]{1,0:T(4,128)} %row_ref.1) | copy-start | bytes 1492
  4.9 0.7 %copy-start.4 = (f32[4,31]{1,0:T(4,128)S(1)}, f32[4,31]{1,0:T(4,128)}, u32[]{:S(2)}) copy-start(f32[4,31]{1,0:T(4,128)} %col_ref.1) | copy-start | bytes 1492
  5.6 0.7 %copy-start.5 = (bf16[1,64]{1,0:T(2,128)(2,1)S(1)}, bf16[1,64]{1,0:T(2,128)(2,1)}, u32[]{:S(2)}) copy-start(bf16[1,64]{1,0:T(2,128)(2,1)} %gain_ref.1) | copy-start | bytes 388
  6.2 0.7 %copy-start.6 = (s32[1,64]{1,0:T(1,128)S(1)}, s32[1,64]{1,0:T(1,128)}, u32[]{:S(2)}) copy-start(s32[1,64]{1,0:T(1,128)} %offset_ref.1) | copy-start | bytes 772

commit v2 on v1

--- a/solution.py
+++ b/solution.py
@@ -12,7 +12,8 @@
 BF16 = jnp.bfloat16
 HALO = 16
 PACK = 3
-CHUNK = 8
+TILE = 16
+PIECES = 2
 
 
 def dot(a, b):
@@ -27,16 +28,23 @@
 def kernel(
     tubes,
     blks,
+    latent_hbm,
+    weight_hbm,
+    row_hbm,
+    col_hbm,
+    exposure_hbm,
+    gain_hbm,
+    owner_hbm,
+    offset_hbm,
+    out_ref,
+    exposure_buf,
     latent_ref,
-    weight_ref,
+    weight_own,
     row_ref,
     col_ref,
-    exposure_ref,
     gain_ref,
     owner_ref,
     offset_ref,
-    out_ref,
-    exposure_buf,
     latent_half,
     view,
     side_view,
@@ -45,7 +53,7 @@
     tap_other,
     gain_send,
     gain_recv,
-    mask,
+    pick,
     count_send,
     count_recv,
     row_band,
@@ -62,6 +70,7 @@
     corner_recv,
     total,
     load_sem,
+    small_sem,
     view_send,
     view_recv,
     weight_sem,
@@ -81,10 +90,10 @@
     ext = half + 2 * HALO
     inner = half + HALO
     group = inner // PACK
-    kernels = weight_ref.shape[0]
+    kernels = weight_hbm.shape[0]
     taps = row_ref.shape[1]
     margin = taps // 2
-    slots = exposure_ref.shape[0]
+    slots = exposure_hbm.shape[0]
     t = lax.axis_index("tube")
     b = lax.axis_index("blk")
     s = lax.axis_index("sub")
@@ -115,16 +124,31 @@
             device_id_type=MESH,
         )
 
+    def load(src, dst, n):
+        return pltpu.make_async_copy(src, dst, small_sem.at[n])
+
+    small = [
+        load(owner_hbm, owner_ref, 0),
+        load(offset_hbm, offset_ref, 1),
+        load(gain_hbm, gain_ref, 2),
+        load(row_hbm, row_ref, 3),
+        load(col_hbm, col_ref, 4),
+    ]
+    load_latent = load(latent_hbm, latent_ref, 5)
+    load_weight = load(
+        weight_hbm.at[:, pl.ds(pl.multiple_of(s * half, half), half)], weight_own, 6
+    )
+    piece = half // PIECES
     loads = [
         pltpu.make_async_copy(
-            exposure_ref.at[pl.ds(c * CHUNK, CHUNK)],
-            exposure_buf.at[pl.ds(c * CHUNK, CHUNK)],
-            load_sem.at[c],
-        )
-        for c in range(slots // CHUNK)
+            exposure_hbm.at[:, pl.ds(h * piece, piece)],
+            exposure_buf.at[:, pl.ds(h * piece, piece)],
+            load_sem.at[h],
+        )
+        for h in range(PIECES)
     ]
-    for load in loads:
-        load.start()
+    for copy in small + loads + [load_latent, load_weight]:
+        copy.start()
 
     barrier = pltpu.get_barrier_semaphore()
     near = [0] + list(sides)
@@ -156,119 +180,41 @@
                         device_id_type=MESH,
                     )
 
-    latent_half[...] = latent_ref[...].astype(BF16)
+    for copy in small:
+        copy.wait()
     tap_own[...] = jnp.zeros_like(tap_own)
     tap_own[0:kernels, 0:taps] = row_ref[...]
     tap_own[kernels : 2 * kernels, 0:taps] = col_ref[...]
-    eye = lax.broadcasted_iota(jnp.int32, (slots, slots), 0) == lax.broadcasted_iota(
-        jnp.int32, (slots, slots), 1
-    )
-    offset = jnp.sum(
-        jnp.where(eye, jnp.broadcast_to(offset_ref[...].astype(F32), (slots, slots)), 0.0),
-        axis=1,
-        keepdims=True,
-    )
-    gain = jnp.sum(
-        jnp.where(eye, jnp.broadcast_to(gain_ref[...].astype(F32), (slots, slots)), 0.0),
-        axis=1,
-        keepdims=True,
-    )
-    owner = owner_ref[...].astype(F32)
+    place = (owner_ref[...] * 2 + offset_ref[...]).astype(F32)
+    gain = gain_ref[...].astype(F32)
     here = s.astype(F32)
     for p in range(tubes):
-        hit = jnp.where((owner == float(p)) & (offset == here), 1.0, 0.0)
-        mask[p] = jnp.broadcast_to(hit, (slots, block))
-        gain_send[p] = jnp.broadcast_to(jnp.sum(hit * gain, axis=0, keepdims=True), (8, block))
-
-    pl.semaphore_wait(
-        barrier,
-        fixed + extra * ((t > 0).astype(jnp.int32) + (t < tubes - 1).astype(jnp.int32)),
+        hit = jnp.where(place == here + float(2 * p), gain, 0.0)
+        gain_send[p] = jnp.broadcast_to(jnp.sum(hit, axis=1, keepdims=True), (8, block))
+
+    depth = slots * TILE
+    slot_of = lax.broadcasted_iota(jnp.int32, (slots, depth), 1) // TILE
+    expand = jnp.where(slot_of == lax.broadcasted_iota(jnp.int32, (slots, depth), 0), 1.0, 0.0)
+    wide = dot(jnp.broadcast_to(place, (8, slots)).astype(BF16), expand.astype(BF16))[0:1] - here
+    same = lax.broadcasted_iota(jnp.int32, (TILE, depth), 1) % TILE == lax.broadcasted_iota(
+        jnp.int32, (TILE, depth), 0
     )
-
-    tap_copy = remote(tap_own, tap_other, tap_sem.at[0], tap_sem.at[1], at(sub=o))
-    tap_copy.start()
-    weight_copy = remote(
-        weight_ref.at[:, pl.ds(o * half, half)],
-        weight_other,
-        weight_sem.at[0],
-        weight_sem.at[1],
-        at(sub=o),
-    )
-    weight_copy.start()
-    gain_copies = []
-    for j in range(1, tubes):
-        p = lax.rem(t + j, tubes)
-        gain_copies.append(
-            remote(gain_send.at[p], gain_recv.at[j - 1], gain_ssem.at[j - 1], gain_rsem.at[j - 1], at(tube=p))
-        )
-        gain_copies[-1].start()
-    own_rows = pl.ds(pl.multiple_of(s * (rows - inner), HALO), inner)
-    own_place = pl.ds(pl.multiple_of(o * HALO, HALO), inner)
-    edge_rows = pl.ds(pl.multiple_of(o * (rows - HALO), HALO), HALO)
-    edge_place = pl.ds(pl.multiple_of(s * inner, HALO), HALO)
-    edge_copies = [
-        remote(
-            latent_half.at[edge_rows],
-            view.at[edge_place],
-            view_send.at[0],
-            view_recv.at[0],
-            at(tube=ahead),
-        )
-    ]
-    side_copies = []
-    for i, step in enumerate(sides):
-        side_copies.append(
-            remote(
-                latent_half.at[own_rows],
-                side_view.at[i, own_place],
-                view_send.at[1 + 2 * i],
-                view_recv.at[1 + 2 * i],
-                at(blk=blk_at(step)),
-            )
-        )
-        edge_copies.append(
-            remote(
-                latent_half.at[edge_rows],
-                side_view.at[i, edge_place],
-                view_send.at[2 + 2 * i],
-                view_recv.at[2 + 2 * i],
-                at(tube=ahead, blk=blk_at(step)),
-            )
-        )
-    for copy in side_copies:
-        copy.start()
-
-    @pl.when(has_ahead)
-    def _():
-        for copy in edge_copies:
-            copy.start()
-
-    view[own_place, :] = latent_half[own_rows, :]
-    piece = half // 2
+    for p in range(tubes):
+        pick[p * TILE : (p + 1) * TILE, :] = jnp.where(
+            same & (wide == float(2 * p)), 1.0, 0.0
+        ).astype(BF16)
+
+    def count_piece(h):
+        loads[h].wait()
+        for g in range(h * piece // TILE, (h + 1) * piece // TILE):
+            part = slice(g * TILE, (g + 1) * TILE)
+            sums = dot(pick[...], exposure_buf[:, part, :].reshape(depth, block)).astype(BF16)
+            for p in range(tubes):
+                count_send[p, part, :] = sums[p * TILE : (p + 1) * TILE]
+
     count_copies = []
-    for h in range(2):
-        for low in range(0, tubes, 4):
-            places = range(low, min(low + 4, tubes))
-
-            def add(c, accs, h=h, places=places, wait=(h == 0 and low == 0)):
-                base = pl.multiple_of(c * CHUNK, CHUNK)
-                if wait:
-                    pltpu.make_async_copy(
-                        exposure_ref.at[pl.ds(base, CHUNK)],
-                        exposure_buf.at[pl.ds(base, CHUNK)],
-                        load_sem.at[c],
-                    ).wait()
-                picks = [mask[p, pl.ds(base, CHUNK), :] for p in places]
-                for q in range(CHUNK):
-                    value = exposure_buf[base + q, h * piece : (h + 1) * piece, :].astype(F32)
-                    accs = tuple(a + m[q : q + 1, :] * value for a, m in zip(accs, picks))
-                return accs
-
-            sums = lax.fori_loop(
-                0, slots // CHUNK, add, tuple(jnp.zeros((piece, block), F32) for _ in places)
-            )
-            for p, value in zip(places, sums):
-                count_send[p, h * piece : (h + 1) * piece, :] = value.astype(BF16)
+
+    def send_piece(h):
         for j in range(1, tubes):
             p = lax.rem(t + j, tubes)
             part = pl.ds(h * piece, piece)
@@ -283,13 +229,86 @@
             )
             count_copies[-1].start()
 
-    tap_copy.wait()
+    count_piece(0)
+    pl.semaphore_wait(
+        barrier,
+        fixed + extra * ((t > 0).astype(jnp.int32) + (t < tubes - 1).astype(jnp.int32)),
+    )
+    send_piece(0)
+
+    tap_copy = remote(tap_own, tap_other, tap_sem.at[0], tap_sem.at[1], at(sub=o))
+    tap_copy.start()
+    weight_copy = remote(
+        weight_hbm.at[:, pl.ds(pl.multiple_of(o * half, half), half)],
+        weight_other,
+        weight_sem.at[0],
+        weight_sem.at[1],
+        at(sub=o),
+    )
+    weight_copy.start()
+    gain_copies = []
+    for j in range(1, tubes):
+        p = lax.rem(t + j, tubes)
+        gain_copies.append(
+            remote(gain_send.at[p], gain_recv.at[j - 1], gain_ssem.at[j - 1], gain_rsem.at[j - 1], at(tube=p))
+        )
+        gain_copies[-1].start()
+    load_latent.wait()
+    latent_half[...] = latent_ref[...].astype(BF16)
+    own_rows = pl.ds(pl.multiple_of(s * (rows - inner), HALO), inner)
+    own_place = pl.ds(pl.multiple_of(o * HALO, HALO), inner)
+    edge_rows = pl.ds(pl.multiple_of(o * (rows - HALO), HALO), HALO)
+    edge_place = pl.ds(pl.multiple_of(s * inner, HALO), HALO)
+    edge_copies = [
+        remote(
+            latent_half.at[edge_rows],
+            view.at[edge_place],
+            view_send.at[0],
+            view_recv.at[0],
+            at(tube=ahead),
+        )
+    ]
+    side_copies = []
+    for i, step in enumerate(sides):
+        side_copies.append(
+            remote(
+                latent_half.at[own_rows],
+                side_view.at[i, own_place],
+                view_send.at[1 + 2 * i],
+                view_recv.at[1 + 2 * i],
+                at(blk=blk_at(step)),
+            )
+        )
+        edge_copies.append(
+            remote(
+                latent_half.at[edge_rows],
+                side_view.at[i, edge_place],
+                view_send.at[2 + 2 * i],
+                view_recv.at[2 + 2 * i],
+                at(tube=ahead, blk=blk_at(step)),
+            )
+        )
+    for copy in side_copies:
+        copy.start()
+
+    @pl.when(has_ahead)
+    def _():
+        for copy in edge_copies:
+            copy.start()
+
+    view[own_place, :] = latent_half[own_rows, :]
+    for h in range(1, PIECES):
+        count_piece(h)
+        send_piece(h)
+
+    load_weight.wait()
     for i, ref in enumerate((tap_own, tap_other)):
+        if i == 1:
+            tap_copy.wait()
+            weight_copy.wait()
         rounded = ref[...].astype(BF16).astype(F32)
         sums = jnp.sum(rounded, axis=1, keepdims=True)
         scale = 1.0 / (sums[0:kernels] * sums[kernels : 2 * kernels])
-        if i == 1:
-            weight_copy.wait()
         for k in range(kernels):
             n = i * kernels + k
             along = band(rounded[k : k + 1], HALO - margin, half)
@@ -297,10 +316,7 @@
             row_band[n] = along.astype(BF16)
             row_band_t[:, n * half : (n + 1) * half] = along.T[0:ext].astype(BF16)
             col_band[n] = around.astype(BF16)
-            if i == 0:
-                own = weight_ref[k, pl.ds(pl.multiple_of(s * half, half), half), :]
-            else:
-                own = weight_other[k]
+            own = weight_own[k] if i == 0 else weight_other[k]
             scaled[n] = own.astype(F32) * scale[k : k + 1]
 
     def adjoint(factor):
@@ -474,14 +490,23 @@
     nside = 1 if blks == 2 else 2
     peers = tubes - 1
     vmem = pl.BlockSpec(memory_space=pltpu.VMEM)
+    anywhere = pl.BlockSpec(memory_space=pl.ANY)
+    taps = row_taps.shape[1]
     dma = pltpu.SemaphoreType.DMA
     return pl.pallas_call(
         functools.partial(kernel, tubes, blks),
         out_shape=jax.ShapeDtypeStruct((rows, block), F32),
-        in_specs=[vmem] * 4 + [pl.BlockSpec(memory_space=pl.ANY)] + [vmem] * 3,
+        in_specs=[anywhere] * 8,
         out_specs=vmem,
         scratch_shapes=[
             pltpu.VMEM((slots, block, block), BF16),
+            pltpu.VMEM((rows, block), F32),
+            pltpu.VMEM((kernels, half, block), BF16),
+            pltpu.VMEM((kernels, taps), F32),
+            pltpu.VMEM((kernels, taps), F32),
+            pltpu.VMEM((1, slots), BF16),
+            pltpu.VMEM((1, slots), jnp.int32),
+            pltpu.VMEM((1, slots), jnp.int32),
             pltpu.VMEM((rows, block), BF16),
             pltpu.VMEM((ext, block), BF16),
             pltpu.VMEM((nside, ext, block), BF16),
@@ -490,7 +515,7 @@
             pltpu.VMEM((2 * kernels, 2 * block), F32),
             pltpu.VMEM((tubes, 8, block), F32),
             pltpu.VMEM((peers, 8, block), F32),
-            pltpu.VMEM((tubes, slots, block), F32),
+            pltpu.VMEM((tubes * TILE, slots * TILE), BF16),
             pltpu.VMEM((tubes, half, block), BF16),
             pltpu.VMEM((peers, half, block), BF16),
             pltpu.VMEM((2 * kernels, half, 2 * block), BF16),
@@ -506,15 +531,16 @@
             pltpu.VMEM((2, nside, 2, inner // PACK, block), F32),
             pltpu.VMEM((2, nside, 2, HALO, block), F32),
             pltpu.VMEM((2, rows, block), F32),
-            dma((slots // CHUNK,)),
+            dma((PIECES,)),
+            dma((7,)),
             dma((1 + 2 * nside,)),
             dma((1 + 2 * nside,)),
             dma((2,)),
             dma((2,)),
             dma((peers,)),
             dma((peers,)),
-            dma((2, peers)),
-            dma((2, peers)),
+            dma((PIECES, peers)),
+            dma((PIECES, peers)),
             dma((2, 4 * nside + 3)),
             dma((2,)),
             dma((2, 2)),
@@ -522,9 +548,9 @@
             dma((2, nside, 2)),
         ],
         compiler_params=pltpu.CompilerParams(
-            collective_id=0, has_side_effects=True, vmem_limit_bytes=40 * 1024 * 1024
+            collective_id=0, has_side_effects=True, vmem_limit_bytes=60 * 1024 * 1024
         ),
-    )(latent, weight_maps, row_taps, col_taps, exposures[0], gains, owners[0], offsets)
+    )(latent, weight_maps, row_taps, col_taps, exposures[0], gains, owners.reshape(1, slots), offsets)
 
 
 def solution(mesh):

time: 25.6 us -> 20.9 us (0.82)
  local copies, waits for them, and re-layouts: 7.52 us -> 1.57 us
  Pallas kernels: 17.8 us -> 19.2 us
    unnamed x15 -> x1, local copies, waits for them, and re-layouts: 6.77 us -> 1.57 us
    pallas_call x1, Pallas kernels: 17.8 us -> 19.2 us  [body(): pl.pallas_call(functools.partial(kernel, tubes, blks), out_shape=jax.Shap...]
    squeeze x1 -> x0, local copies, waits for them, and re-layouts: 0.74 us -> none  [body(): owners[0]]
where the time goes in v2:
time: 20.9 us; the launch traced here: 20.7 us
  Pallas kernels  19.2 us (92%)
  local copies, waits for them, and re-layouts  1.57 us (8%)
    pallas_call x1, Pallas kernels, body(): pl.pallas_call(functools.partial(kernel, tubes, blks), out_shape=jax.Shap...  19.2 us
    unnamed x1, local copies, waits for them, and re-layouts  1.57 us

profile of v2, /device:TPU:0, one launch (start us, length us, event | category | flops | bytes accessed | tf_op | source)
XLA Modules:
  0.0 20.7 jit_solution(11312352137487739821)
XLA Ops:
  0.0 19.2 %shard_map.82 = f32[256,128]{1,0:T(8,128)} custom-call(f32[256,128]{1,0:T(8,128)} %latent_hbm.1, bf16[4,256,128]{2,1,0:T(8,128)(2,1)} %weight_hbm.1, f32[4,31]{1,0:T(4,128)} %row_hbm.1, f32[4,31]{1,0:T(4,128)} %col_hbm.1, bf16[64,128,128]{2,1,0:T(8,128)(2,1)} %bitcast.2, bf16[1,64]{1,0:T(2,128)(2,1)} %gain_hbm.1, s32[1,64]{1,0:T(1,128)} %bitcast.3, ...), custom_call_target="tpu_custom_call" | custom-call | tf_op jit(solution)/shard_map/pallas_call | solution.py:496
  19.2 1.6 %copy.10 = f32[256,128]{1,0:T(8,128)} copy(f32[256,128]{1,0:T(8,128)} %shard_map.82) | data formatting | bytes 262144

commit v3 on v2

--- a/solution.py
+++ b/solution.py
@@ -416,6 +416,12 @@
                     value = value + jnp.where(lanes_of[i], corner_recv[f, i, n], 0.0)
                 total[f, start : start + HALO, :] += value
 
+    coverage = gain_send[t]
+    for j, copy in enumerate(gain_copies):
+        copy.wait()
+        coverage = coverage + gain_recv[j]
+    sent_d = exchange(0, adjoint(None) * coverage[0:1, 0:1])
+
     for copy in side_copies:
         copy.wait_recv()
 
@@ -445,20 +451,13 @@
         blurred = blurred + scaled[n] * both
     inverse = 1.0 / blurred
 
-    coverage = gain_send[t]
-    for j, copy in enumerate(gain_copies):
-        copy.wait()
-        coverage = coverage + gain_recv[j]
-    sent_d = exchange(0, adjoint(None) * coverage[0:1, 0:1])
-    counts_own = count_send[t].astype(F32)
-    collect(0)
-
     for copy in count_copies:
         copy.wait()
-    counts = counts_own
+    counts = count_send[t].astype(F32)
     for j in range(tubes - 1):
         counts = counts + count_recv[j].astype(F32)
     sent_n = exchange(1, adjoint(counts * inverse))
+    collect(0)
     collect(1)
     out_ref[...] = latent_ref[...] * total[1] / jnp.maximum(total[0], 0.25)
 

time: 20.9 us -> 17.8 us (0.85)
  Pallas kernels: 19.2 us -> 16.1 us
    pallas_call x1, Pallas kernels: 19.2 us -> 16.1 us  [body(): pl.pallas_call(functools.partial(kernel, tubes, blks), out_shape=jax.Shap...]
where the time goes in v3:
time: 17.8 us; the launch traced here: 17.6 us
  Pallas kernels  16.1 us (90%)
  local copies, waits for them, and re-layouts  1.57 us (9%)
    pallas_call x1, Pallas kernels, body(): pl.pallas_call(functools.partial(kernel, tubes, blks), out_shape=jax.Shap...  16.1 us
    unnamed x1, local copies, waits for them, and re-layouts  1.57 us

profile of v3, /device:TPU:0, one launch (start us, length us, event | category | flops | bytes accessed | tf_op | source)
XLA Modules:
  0.0 17.6 jit_solution(14779485776559860475)
XLA Ops:
  0.0 16.1 %shard_map.82 = f32[256,128]{1,0:T(8,128)} custom-call(f32[256,128]{1,0:T(8,128)} %latent_hbm.1, bf16[4,256,128]{2,1,0:T(8,128)(2,1)} %weight_hbm.1, f32[4,31]{1,0:T(4,128)} %row_hbm.1, f32[4,31]{1,0:T(4,128)} %col_hbm.1, bf16[64,128,128]{2,1,0:T(8,128)(2,1)} %bitcast.2, bf16[1,64]{1,0:T(2,128)(2,1)} %gain_hbm.1, s32[1,64]{1,0:T(1,128)} %bitcast.3, ...), custom_call_target="tpu_custom_call" | custom-call | tf_op jit(solution)/shard_map/pallas_call | solution.py:495
  16.1 1.6 %copy.10 = f32[256,128]{1,0:T(8,128)} copy(f32[256,128]{1,0:T(8,128)} %shard_map.82) | data formatting | bytes 262144

commit v4 on v2

--- a/solution.py
+++ b/solution.py
@@ -13,7 +13,7 @@
 HALO = 16
 PACK = 3
 TILE = 16
-PIECES = 2
+PIECES = 4
 
 
 def dot(a, b):
@@ -124,6 +124,36 @@
             device_id_type=MESH,
         )
 
+    barrier = pltpu.get_barrier_semaphore()
+    near = [0] + list(sides)
+    fixed = 0
+    for step in near:
+        for sub in (s, o):
+            if step == 0 and sub is s:
+                continue
+            pl.semaphore_signal(barrier, inc=1, device_id=at(blk=blk_at(step), sub=sub), device_id_type=MESH)
+            fixed += 1
+    for j in range(1, tubes):
+        pl.semaphore_signal(
+            barrier, inc=1, device_id=at(tube=lax.rem(t + j, tubes)), device_id_type=MESH
+        )
+        fixed += 1
+    extra = 2 * len(near) - 1
+    for beside in (t - 1, t + 1):
+
+        @pl.when((beside >= 0) & (beside < tubes))
+        def _():
+            for step in near:
+                for sub in (s, o):
+                    if step == 0 and sub is s:
+                        continue
+                    pl.semaphore_signal(
+                        barrier,
+                        inc=1,
+                        device_id=at(tube=beside, blk=blk_at(step), sub=sub),
+                        device_id_type=MESH,
+                    )
+
     def load(src, dst, n):
         return pltpu.make_async_copy(src, dst, small_sem.at[n])
 
@@ -150,36 +180,6 @@
     for copy in small + loads + [load_latent, load_weight]:
         copy.start()
 
-    barrier = pltpu.get_barrier_semaphore()
-    near = [0] + list(sides)
-    fixed = 0
-    for step in near:
-        for sub in (s, o):
-            if step == 0 and sub is s:
-                continue
-            pl.semaphore_signal(barrier, inc=1, device_id=at(blk=blk_at(step), sub=sub), device_id_type=MESH)
-            fixed += 1
-    for j in range(1, tubes):
-        pl.semaphore_signal(
-            barrier, inc=1, device_id=at(tube=lax.rem(t + j, tubes)), device_id_type=MESH
-        )
-        fixed += 1
-    extra = 2 * len(near) - 1
-    for beside in (t - 1, t + 1):
-
-        @pl.when((beside >= 0) & (beside < tubes))
-        def _():
-            for step in near:
-                for sub in (s, o):
-                    if step == 0 and sub is s:
-                        continue
-                    pl.semaphore_signal(
-                        barrier,
-                        inc=1,
-                        device_id=at(tube=beside, blk=blk_at(step), sub=sub),
-                        device_id_type=MESH,
-                    )
-
     for copy in small:
         copy.wait()
     tap_own[...] = jnp.zeros_like(tap_own)
@@ -212,7 +212,7 @@
             for p in range(tubes):
                 count_send[p, part, :] = sums[p * TILE : (p + 1) * TILE]
 
-    count_copies = []
+    count_copies, gain_copies = [], []
 
     def send_piece(h):
         for j in range(1, tubes):
@@ -234,6 +234,12 @@
         barrier,
         fixed + extra * ((t > 0).astype(jnp.int32) + (t < tubes - 1).astype(jnp.int32)),
     )
+    for j in range(1, tubes):
+        p = lax.rem(t + j, tubes)
+        gain_copies.append(
+            remote(gain_send.at[p], gain_recv.at[j - 1], gain_ssem.at[j - 1], gain_rsem.at[j - 1], at(tube=p))
+        )
+        gain_copies[-1].start()
     send_piece(0)
 
     tap_copy = remote(tap_own, tap_other, tap_sem.at[0], tap_sem.at[1], at(sub=o))
@@ -246,13 +252,6 @@
         at(sub=o),
     )
     weight_copy.start()
-    gain_copies = []
-    for j in range(1, tubes):
-        p = lax.rem(t + j, tubes)
-        gain_copies.append(
-            remote(gain_send.at[p], gain_recv.at[j - 1], gain_ssem.at[j - 1], gain_rsem.at[j - 1], at(tube=p))
-        )
-        gain_copies[-1].start()
     load_latent.wait()
     latent_half[...] = latent_ref[...].astype(BF16)
     own_rows = pl.ds(pl.multiple_of(s * (rows - inner), HALO), inner)
@@ -334,13 +333,6 @@
     def exchange(f, value):
         main_send[f] = value[:, 0:block]
         strip_send[f] = value[:, block : 2 * block]
-        packed = jnp.zeros((group, block), F32)
-        start = pl.multiple_of(o * HALO, HALO)
-        for g in range(PACK):
-            packed = packed + pltpu.roll(
-                strip_send[f, pl.ds(start + g * group, group), :], HALO + 2 * HALO * g, 1
-            )
-        packed_send[f] = packed
         copies, edges = [], []
         count = 0
 
@@ -374,14 +366,20 @@
                 at(tube=behind, sub=sub),
             )
         add(copies, main_send.at[f, own_place], main_recv.at[f], main_rsem.at[f], at(sub=o))
-        for copy in copies:
-            copy.start()
-
         @pl.when(has_behind)
         def _():
             for copy in edges:
                 copy.start()
 
+        packed = jnp.zeros((group, block), F32)
+        start = pl.multiple_of(o * HALO, HALO)
+        for g in range(PACK):
+            packed = packed + pltpu.roll(
+                strip_send[f, pl.ds(start + g * group, group), :], HALO + 2 * HALO * g, 1
+            )
+        packed_send[f] = packed
+        for copy in copies:
+            copy.start()
         return copies, edges
 
     def landed(buf, rsem):
@@ -416,6 +414,8 @@
                     value = value + jnp.where(lanes_of[i], corner_recv[f, i, n], 0.0)
                 total[f, start : start + HALO, :] += value
 
+    spread_d = adjoint(None)
+
     for copy in side_copies:
         copy.wait_recv()
 
@@ -449,16 +449,15 @@
     for j, copy in enumerate(gain_copies):
         copy.wait()
         coverage = coverage + gain_recv[j]
-    sent_d = exchange(0, adjoint(None) * coverage[0:1, 0:1])
-    counts_own = count_send[t].astype(F32)
-    collect(0)
+    sent_d = exchange(0, spread_d * coverage[0:1, 0:1])
 
     for copy in count_copies:
         copy.wait()
-    counts = counts_own
+    counts = count_send[t].astype(F32)
     for j in range(tubes - 1):
         counts = counts + count_recv[j].astype(F32)
     sent_n = exchange(1, adjoint(counts * inverse))
+    collect(0)
     collect(1)
     out_ref[...] = latent_ref[...] * total[1] / jnp.maximum(total[0], 0.25)
 

time: 20.9 us -> 17.1 us (0.82)
  Pallas kernels: 19.2 us -> 15.4 us
    pallas_call x1, Pallas kernels: 19.2 us -> 15.4 us  [body(): pl.pallas_call(functools.partial(kernel, tubes, blks), out_shape=jax.Shap...]
where the time goes in v4:
time: 17.1 us; the launch traced here: 16.9 us
  Pallas kernels  15.4 us (90%)
  local copies, waits for them, and re-layouts  1.57 us (9%)
    pallas_call x1, Pallas kernels, body(): pl.pallas_call(functools.partial(kernel, tubes, blks), out_shape=jax.Shap...  15.4 us
    unnamed x1, local copies, waits for them, and re-layouts  1.57 us

profile of v4, /device:TPU:0, one launch (start us, length us, event | category | flops | bytes accessed | tf_op | source)
XLA Modules:
  0.0 16.9 jit_solution(10282228052073146678)
XLA Ops:
  0.0 15.4 %shard_map.82 = f32[256,128]{1,0:T(8,128)} custom-call(f32[256,128]{1,0:T(8,128)} %latent_hbm.1, bf16[4,256,128]{2,1,0:T(8,128)(2,1)} %weight_hbm.1, f32[4,31]{1,0:T(4,128)} %row_hbm.1, f32[4,31]{1,0:T(4,128)} %col_hbm.1, bf16[64,128,128]{2,1,0:T(8,128)(2,1)} %bitcast.2, bf16[1,64]{1,0:T(2,128)(2,1)} %gain_hbm.1, s32[1,64]{1,0:T(1,128)} %bitcast.3, ...), custom_call_target="tpu_custom_call" | custom-call | tf_op jit(solution)/shard_map/pallas_call | solution.py:495
  15.4 1.6 %copy.10 = f32[256,128]{1,0:T(8,128)} copy(f32[256,128]{1,0:T(8,128)} %shard_map.82) | data formatting | bytes 262144
